TPU v7x, 256 devices: a whole 4x4x8 slice. The times are simulated.
256 devices in a mesh: seq: 64 (over z_lo, y, x, core), grp: 4 (over z_hi).
Axes of the slice: x: 4, y: 4, z: 8 (z_hi: 4, z_lo: 2; z = z_hi * 2 + z_lo), core: 2. Of those that a mesh axis runs over, the one named last changes fastest.
Arguments:
- candidates: bfloat16 [64, 128, 128], P('grp', 'seq'), may hold values from -6 to 6
- behav_keys: bfloat16 [64, 65536, 128], P('grp', 'seq'), may hold values from -100 to 100
- behav_values: bfloat16 [64, 65536, 128], P('grp', 'seq'), may hold values from -6 to 6
- w_query: bfloat16 [128, 128], replicated, may hold values from -0.5 to 0.5
- w_hidden: bfloat16 [256, 1024], replicated, may hold values from -0.375 to 0.375
- w_out: float32 [1024], replicated, may hold values from -0.1875 to 0.1875
- clicks: int32 [64, 128], P('grp', 'seq'), may hold values 0 or 1
Outputs:
- logits: float32 [64, 128], P('grp', 'seq')
- grad_hidden: float32 [256, 1024], replicated
- grad_out: float32 [1024], replicated
All inputs are finite; a program needn't handle non-finite values. No bound on the sum of `clicks` on one device may be relied on, other than what follows from the above.
Results may differ from a plain program's by a relative error of at most 0.0065.
The roundings to bfloat16 on the way count: a program that leaves them out, or rounds other values in their place, can miss the bound.
Values may be sent and summed in bfloat16 or wider, within the bound.
A program may use at most 64 MiB of HBM per device.

v0:
```python
import functools
import math

import jax
import jax.numpy as jnp
from jax import lax
from jax.experimental import pallas as pl
from jax.experimental.pallas import tpu as pltpu
from jax.sharding import PartitionSpec as P

HEADS = 4
MESH = pl.DeviceIdType.MESH
NT = (((1,), (1,)), ((), ()))
F32 = jnp.float32
BF16 = jnp.bfloat16
GATHER, GATHER_TWIN, PARTIAL, TWIN_HEAD, OUT_X, LOGITS, OUT_GRP, OUT_ZY, OUT_TWIN = 0, 2, 4, 5, 6, 7, 8, 9, 10
REDUCE, GRP, ALL, ALL_TWIN = 11, 13, 15, 17
PHASES = 19
CHUNK = 512


def kernel(
    nc,
    ng,
    cand_hbm,
    keys_hbm,
    vals_hbm,
    wq_hbm,
    wh_hbm,
    wout_hbm,
    clicks_hbm,
    logits_ref,
    gh_ref,
    go_ref,
    x_buf,
    xf,
    qf,
    k_buf,
    v_buf,
    s_even,
    s_odd,
    q_heads,
    wq_buf,
    wh_buf,
    wout_ref,
    clicks_ref,
    clk,
    mine,
    theirs,
    p_send,
    p_recv,
    h_send,
    h_recv,
    g_send,
    g_recv,
    z_buf,
    ga_buf,
    l_send,
    l_recv,
    o1,
    o2,
    o3,
    o4,
    kv_sems,
    w_sems,
    twin_sems,
    twin_send_sem,
    send_sems,
    recv_sems,
):
    me = lax.axis_index("seq")
    grp = lax.axis_index("grp")
    core = lax.rem(me, 2)
    chip = me // 2
    users, length, width = k_buf.shape
    half_users = users // 2
    u_me = me // 4
    c_me = lax.rem(chip, 2)
    first_half = 1 - u_me // half_users
    head_size = width // HEADS
    scale = math.log2(math.e) / math.sqrt(head_size)
    hw = HEADS * width

    def user_at(t):
        return lax.rem(first_half + t // half_users, 2) * half_users + lax.rem(
            u_me + 1 + t, half_users
        )

    def on_chip(k):
        return lax.rem(chip + k, nc)

    def remote(src, dst, phase, seq, group=None):
        where = {"seq": seq} if group is None else {"seq": seq, "grp": group}
        return pltpu.make_async_remote_copy(
            src_ref=src,
            dst_ref=dst,
            send_sem=send_sems.at[phase],
            recv_sem=recv_sems.at[phase],
            device_id=where,
            device_id_type=MESH,
        )

    twin = chip * 2 + 1 - core

    def same_core(other_chip):
        return other_chip * 2 + core

    def local(src, dst, sem):
        return pltpu.make_async_copy(src, dst, sem)

    def wait_send(ref, phase):
        local(ref, ref, send_sems.at[phase]).wait()

    def wait_recv(ref, phase):
        local(ref, ref, recv_sems.at[phase]).wait()

    own_loads = [
        local(cand_hbm.at[pl.ds(16 * i, 16)], x_buf.at[i, core * nc + chip], w_sems.at[i])
        for i in range(2)
    ]
    for load in own_loads:
        load.start()
    wq_load = local(wq_hbm, wq_buf, w_sems.at[2])
    wq_load.start()
    clicks_load = local(clicks_hbm, clicks_ref, w_sems.at[4])
    clicks_load.start()

    @pl.loop(0, users)
    def _(t):
        u = user_at(t)
        local(keys_hbm.at[u], k_buf.at[u], kv_sems.at[0, t]).start()
        local(vals_hbm.at[u], v_buf.at[u], kv_sems.at[1, t]).start()

    wh_load = local(wh_hbm, wh_buf, w_sems.at[3])
    wh_load.start()
    wout_load = local(wout_hbm, wout_ref, w_sems.at[5])
    wout_load.start()

    barrier = pltpu.get_barrier_semaphore()
    pl.semaphore_signal(barrier, inc=1, device_id={"seq": twin}, device_id_type=MESH)

    @pl.loop(1, nc)
    def _(k):
        pl.semaphore_signal(
            barrier, inc=1, device_id={"seq": same_core(on_chip(k))}, device_id_type=MESH
        )

    for k in range(1, ng):
        pl.semaphore_signal(
            barrier,
            inc=1,
            device_id={"seq": me, "grp": lax.rem(grp + k, ng)},
            device_id_type=MESH,
        )

    clicks_load.wait()
    row_u = lax.broadcasted_iota(jnp.int32, (users, users), 0)
    col_u = lax.broadcasted_iota(jnp.int32, (users, users), 1)
    for c in range(2):
        wide = jnp.broadcast_to(clicks_ref[c : c + 1, :].astype(F32), (users, users))
        column = jnp.sum(jnp.where(row_u == col_u, wide, 0.0), axis=1, keepdims=True)
        clk[c] = jnp.broadcast_to(column, (users, width))

    pl.semaphore_wait(barrier, nc + ng - 1)

    for load in own_loads:
        load.wait()
    own = core * nc + chip

    def send_candidates(turn):
        @pl.loop(1, nc)
        def _(k):
            to = on_chip(k)
            part = lax.rem(to // (nc // 2) + 1 + turn, 2)
            remote(
                x_buf.at[part, own], x_buf.at[part, own], GATHER + part, same_core(to)
            ).start()

    send_candidates(0)

    def pass_on(part):
        wait_recv(x_buf.at[0, pl.ds(0, nc - 1)], GATHER + part)
        block = x_buf.at[part, pl.ds(core * nc, nc)]
        remote(block, block, GATHER_TWIN + part, twin).start()

    def make_queries(part):
        wait_recv(x_buf.at[0, pl.ds(0, nc)], GATHER_TWIN + part)
        x_all = x_buf[part].reshape(2 * nc * 16, width)
        queries = jnp.dot(x_all, wq_buf[...], preferred_element_type=F32)
        qf[part] = queries.astype(BF16).astype(F32)

    second_half = 1 - first_half
    wq_load.wait()
    pass_on(first_half)
    send_candidates(1)
    make_queries(first_half)

    head_of = lax.broadcasted_iota(jnp.int32, (2 * nc, width), 1) // head_size
    lane8 = lax.broadcasted_iota(jnp.int32, (8, width), 1)
    row8 = lax.broadcasted_iota(jnp.int32, (8, width), 0)
    group8 = lax.rem(lane8, head_size) // 8
    is_lse = lax.rem(lane8, 8) == 0
    is_click = lax.rem(lane8, 8) == 1
    at_me = (row8 == lax.rem(chip, 8)) & (group8 == chip // 8) & is_click

    def set_queries(u):
        part = u // half_users
        for c in range(2):
            rows = qf[part, pl.ds(lax.rem(u, half_users) * 2 + c, 2 * nc, stride=16), :]
            for h in range(HEADS):
                first = h * width + c * 2 * nc
                q_heads[first : first + 2 * nc, :] = jnp.where(head_of == h, rows, 0.0).astype(
                    BF16
                )

    def scores(u, j, s_ref, highest):
        rows = slice(j * CHUNK, j * CHUNK + CHUNK)
        s = lax.dot_general(k_buf[u, rows, :], q_heads[...], NT, preferred_element_type=F32)
        s_ref[rows, :] = s
        return jnp.maximum(highest, jnp.max(s.reshape(CHUNK // 8, 8, hw), axis=0))

    lowest = jnp.full((8, hw), -jnp.inf, F32)

    def attend(t, s_ref, s_next, highest, more=True):
        u = user_at(t)
        top = jnp.max(highest, axis=0, keepdims=True) * scale
        local(vals_hbm.at[u], v_buf.at[u], kv_sems.at[1, t]).wait()
        vals = jnp.transpose(v_buf[u])
        if more:
            u_next = user_at(t + 1)
            local(keys_hbm.at[u_next], k_buf.at[u_next], kv_sems.at[0, t + 1]).wait()
            set_queries(u_next)
        highest = lowest
        den = jnp.zeros((8, hw), F32)
        num = [jnp.zeros((2 * head_size, 2 * width), F32) for _ in range(HEADS // 2)]
        for j in range(length // CHUNK):
            if more:
                highest = scores(u_next, j, s_next, highest)
            rows = slice(j * CHUNK, j * CHUNK + CHUNK)
            p = jnp.exp2(s_ref[rows, :] * scale - top)
            den = den + jnp.sum(p.reshape(CHUNK // 8, 8, hw), axis=0)
            probs = p.astype(BF16)
            for h in range(HEADS // 2):
                num[h] = num[h] + jnp.dot(
                    vals[2 * head_size * h : 2 * head_size * (h + 1), rows],
                    probs[:, 2 * width * h : 2 * width * (h + 1)],
                    preferred_element_type=F32,
                )
        den = jnp.sum(den, axis=0, keepdims=True)
        inverse = 1.0 / den
        lse = top + jnp.log2(den)
        att_rows, lse_rows = [], []
        for h in range(HEADS):
            cols = slice(width * h, width * (h + 1))
            sub, at = head_size * (h % 2), width * (h % 2)
            block = num[h // 2][sub : sub + head_size, at : at + width]
            att_rows.append(block * inverse[:, cols])
            lse_rows.append(jnp.broadcast_to(lse[:, cols], (head_size, width)))
        att = jnp.transpose(jnp.concatenate(att_rows, axis=0))
        lse = jnp.transpose(jnp.concatenate(lse_rows, axis=0))
        for c in range(2):
            for half in range(2):
                first = 64 * c + 32 * half
                mine[t, half, c, 0:32] = att[first : first + 32]
                mine[t, half, c, 32:64] = lse[first : first + 32]
        pltpu.make_async_remote_copy(
            src_ref=mine.at[t, 1 - core],
            dst_ref=theirs.at[t],
            send_sem=twin_send_sem,
            recv_sem=twin_sems.at[t],
            device_id={"seq": twin},
            device_id_type=MESH,
        ).start()
        return highest

    def merge(t):
        u = user_at(t)
        local(theirs.at[t], theirs.at[t], twin_sems.at[t]).wait()
        for c in range(2):
            a, b = mine[t, core, c], theirs[t, c]
            top = jnp.maximum(a[32:64], b[32:64])
            wa, wb = jnp.exp2(a[32:64] - top), jnp.exp2(b[32:64] - top)
            total = wa + wb
            lse = top + jnp.log2(total)
            slot = t * 2 + c
            p_send[slot, 0:32] = (a[0:32] * wa + b[0:32] * wb) / total
            tile = jnp.zeros((8, width), F32)
            for g in range(4):
                tile = jnp.where(is_lse & (group8 == g), lse[8 * g : 8 * g + 8], tile)
            click = jnp.broadcast_to(clk[c, pl.ds(u, 1), :], (8, width))
            p_send[slot, 32:40] = jnp.where(at_me, click, tile)
            to = 4 * u + 2 * c + core

            @pl.when(to != me)
            def _():
                remote(p_send.at[slot], p_recv.at[chip], PARTIAL, to).start()

            @pl.when(to == me)
            def _():
                local(p_send.at[slot], p_recv.at[chip], recv_sems.at[PARTIAL]).start()

    u_first = user_at(0)
    local(keys_hbm.at[u_first], k_buf.at[u_first], kv_sems.at[0, 0]).wait()
    set_queries(u_first)
    highest = lowest
    for j in range(length // CHUNK):
        highest = scores(u_first, j, s_even, highest)

    def two_users(i, highest):
        t = 2 * i

        @pl.when(i == half_users // 2 - 1)
        def _():
            pass_on(second_half)

        highest = attend(t, s_even, s_odd, highest)

        @pl.when(i > 0)
        def _():
            merge(t - 1)

        @pl.when(i == half_users // 2 - 1)
        def _():
            make_queries(second_half)
            xf[...] = x_buf[second_half].reshape(2 * nc * 16, width).astype(F32)

        highest = attend(t + 1, s_odd, s_even, highest)
        merge(t)
        return highest

    highest = lax.fori_loop(0, users // 2 - 1, two_users, highest)
    highest = attend(users - 2, s_even, s_odd, highest)
    merge(users - 3)
    attend(users - 1, s_odd, None, highest, more=False)
    merge(users - 2)
    merge(users - 1)

    wait_recv(p_recv, PARTIAL)
    ej = lax.broadcasted_iota(jnp.int32, (width, 4 * width), 0)
    ef = lax.broadcasted_iota(jnp.int32, (width, 4 * width), 1)
    same = (ej // head_size == lax.rem(ef, width) // head_size) & (
        lax.rem(ej, head_size) // 8 == ef // width
    )
    spread = jnp.where(same & (lax.rem(ej, 8) == 0), 1.0, 0.0).astype(BF16)
    spread_click = jnp.where(same & (lax.rem(ej, 8) == 1), 1.0, 0.0).astype(BF16)
    tiles = p_recv[:, 32:40, :]
    rest = tiles.reshape(nc * 8, width)
    lse_all = jnp.zeros((nc * 8, 4 * width), F32)
    for _ in range(3):
        piece = rest.astype(BF16)
        rest = rest - piece.astype(F32)
        lse_all = lse_all + jnp.dot(piece, spread, preferred_element_type=F32)
    lse_all = lse_all.reshape(nc, 8, 4 * width)
    w = jnp.exp2(lse_all - jnp.max(lse_all, axis=0)[None])
    den = jnp.sum(w, axis=0)
    attended = []
    for g in range(4):
        cols = slice(g * width, g * width + width)
        num = jnp.sum(p_recv[:, 8 * g : 8 * g + 8, :] * w[:, :, cols], axis=0)
        attended.append(num / den[:, cols])
    attended = jnp.concatenate(attended, axis=0).astype(BF16).astype(F32)
    click_tile = jnp.where(is_click, jnp.sum(tiles, axis=0), 0.0)
    click = jnp.dot(click_tile.astype(BF16), spread_click, preferred_element_type=F32)
    click = jnp.concatenate([click[:, g * width : g * width + width] for g in range(4)], axis=0)
    click = click[:, 0:1]

    def candidates_of(which):
        first = which * nc * 16 + lax.rem(u_me, half_users) * 2 + c_me
        return xf[pl.ds(first, nc, stride=16), :]

    features = jnp.concatenate([candidates_of(core), attended], axis=1)
    wh_load.wait()
    wout_load.wait()
    pre = jnp.dot(features.astype(BF16), wh_buf[...], preferred_element_type=F32)
    hidden = jnp.maximum(pre, 0.0).astype(BF16).astype(F32)
    logits = jnp.sum(hidden * wout_ref[...], axis=-1, keepdims=True)
    dlogit = 1.0 / (1.0 + jnp.exp(-logits)) - click
    h_send[0:32] = attended
    h_send[32:64] = jnp.broadcast_to(dlogit, (nc, width))
    remote(h_send, h_recv, TWIN_HEAD, twin).start()

    half_hid = wh_buf.shape[1] // 2
    my_cols = pl.ds(pl.multiple_of(core * half_hid, half_hid), half_hid)
    wout = wout_ref[:, my_cols]

    def half_of(a):
        return jnp.where(core == 0, a[:, :half_hid], a[:, half_hid:])

    def dpre_of(pre, dlogit):
        return jnp.where(pre > 0.0, dlogit * wout, 0.0).astype(BF16)

    dpre = dpre_of(half_of(pre), dlogit)
    out_part = jnp.sum(half_of(hidden) * dlogit, axis=0, keepdims=True)
    wait_recv(h_recv, TWIN_HEAD)
    other = jnp.concatenate([candidates_of(1 - core), h_recv[0:32]], axis=1)
    dlogit = h_recv[32:64, 0:1]
    pre = jnp.dot(other.astype(BF16), wh_buf[:, my_cols], preferred_element_type=F32)
    hidden = jnp.maximum(pre, 0.0).astype(BF16).astype(F32)
    out_part = out_part + jnp.sum(hidden * dlogit, axis=0, keepdims=True)
    features = jnp.concatenate([features, other], axis=0)
    dpre = jnp.concatenate([dpre, dpre_of(pre, dlogit)], axis=0)
    grad = jnp.dot(jnp.transpose(features).astype(BF16), dpre, preferred_element_type=F32)
    bw = half_hid // 2
    for part in range(2):
        for b in range(nc):
            i, j = b // 2, b % 2
            first = bw * j + width * part
            g_send[part, b] = grad[16 * i : 16 * i + 16, first : first + width].astype(BF16)

        @pl.loop(1, nc)
        def _(k):
            to = on_chip(k)
            remote(
                g_send.at[part, to], g_recv.at[part, chip], REDUCE + part, same_core(to)
            ).start()

        g_recv[part, chip] = g_send[part, chip]

    at_x, at_zy = lax.rem(chip, 4), chip // 4
    pieces = [out_part[:, width * i : width * i + width] for i in range(4)]
    o1[at_x] = jnp.concatenate(pieces + [jnp.zeros((4, width), F32)], axis=0)
    for k in range(1, 4):
        to = at_zy * 4 + lax.rem(at_x + k, 4)
        remote(o1.at[at_x], o1.at[at_x], OUT_X, same_core(to)).start()

    wide = jnp.broadcast_to(logits, (nc, width))
    for i in range(nc):
        l_send[i] = wide[i : i + 1, :]
    l_slot = c_me * users + u_me

    @pl.loop(1, nc)
    def _(k):
        to = on_chip(k)
        remote(l_send.at[to], l_recv.at[l_slot], LOGITS, same_core(to)).start()

    l_recv[l_slot] = l_send[chip]

    wait_recv(o1.at[pl.ds(0, 3)], OUT_X)
    o2[grp] = o1[0] + o1[1] + o1[2] + o1[3]
    for k in range(1, ng):
        remote(o2.at[grp], o2.at[grp], OUT_GRP, me, lax.rem(grp + k, ng)).start()
    for part in range(2):
        wait_recv(g_recv.at[part, pl.ds(0, nc - 1)], REDUCE + part)
        z_buf[part, grp] = jnp.sum(g_recv[part].astype(F32), axis=0).astype(BF16)
        for k in range(1, ng):
            block = z_buf.at[part, grp]
            remote(block, block, GRP + part, me, lax.rem(grp + k, ng)).start()
    wait_recv(o2.at[pl.ds(0, ng - 1)], OUT_GRP)
    o3[at_zy] = jnp.sum(o2[...], axis=0)
    for k in range(1, 8):
        to = lax.rem(at_zy + k, 8) * 4 + at_x
        remote(o3.at[at_zy], o3.at[at_zy], OUT_ZY, same_core(to)).start()
    for part in range(2):
        wait_recv(z_buf.at[part, pl.ds(0, ng - 1)], GRP + part)
        ga_buf[part, core, chip] = jnp.sum(z_buf[part].astype(F32), axis=0).astype(BF16)

        @pl.loop(1, nc)
        def _(k):
            block = ga_buf.at[part, core, chip]
            remote(block, block, ALL + part, same_core(on_chip(k))).start()

    wait_recv(l_recv.at[pl.ds(0, nc - 1)], LOGITS)
    logit_rows = l_recv[...].reshape(2 * users, width)
    row_o = lax.broadcasted_iota(jnp.int32, (users, width), 0)
    col_o = lax.broadcasted_iota(jnp.int32, (users, width), 1)
    for c in range(2):
        rows = jnp.where(row_o == col_o, logit_rows[users * c : users * (c + 1)], 0.0)
        logits_ref[c : c + 1, :] = jnp.sum(rows, axis=0, keepdims=True)[:, :users]
    wait_recv(o3.at[pl.ds(0, 7)], OUT_ZY)
    o4[core] = jnp.sum(o3[...], axis=0)
    remote(o4.at[core], o4.at[core], OUT_TWIN, twin).start()

    for part in range(2):
        wait_send(x_buf.at[0, pl.ds(0, nc - 1)], GATHER + part)
        wait_send(x_buf.at[0, pl.ds(0, nc)], GATHER_TWIN + part)
    local(theirs, theirs, twin_send_sem).wait()
    wait_send(p_send.at[pl.ds(0, nc - 1)], PARTIAL)
    wait_send(h_send, TWIN_HEAD)
    wait_send(l_send.at[pl.ds(0, nc - 1)], LOGITS)
    for part in range(2):
        wait_send(g_send.at[part, pl.ds(0, nc - 1)], REDUCE + part)
        wait_send(z_buf.at[part, pl.ds(0, ng - 1)], GRP + part)
    wait_send(o1.at[pl.ds(0, 3)], OUT_X)
    wait_send(o2.at[pl.ds(0, ng - 1)], OUT_GRP)
    wait_send(o3.at[pl.ds(0, 7)], OUT_ZY)

    def write(part, side):
        for j in range(2):
            first = side * half_hid + j * bw + part * width
            cols = pl.ds(pl.multiple_of(first, width), width)
            for i in range(nc // 2):
                gh_ref[16 * i : 16 * i + 16, cols] = ga_buf[part, side, 2 * i + j].astype(F32)

    for part in range(2):
        wait_recv(ga_buf.at[part, 0, pl.ds(0, nc - 1)], ALL + part)
        block = ga_buf.at[part, core]
        remote(block, block, ALL_TWIN + part, twin).start()
        write(part, core)
    wait_recv(o4.at[0], OUT_TWIN)
    go_ref[...] = jnp.concatenate([o4[0, 0:4], o4[1, 0:4]], axis=0)
    for part in range(2):
        wait_recv(ga_buf.at[part, 0], ALL_TWIN + part)
        write(part, 1 - core)
    for part in range(2):
        wait_send(ga_buf.at[part, 0, pl.ds(0, nc - 1)], ALL + part)
        wait_send(ga_buf.at[part, 0], ALL_TWIN + part)
    wait_send(o4.at[0], OUT_TWIN)


def on_device(ns, ng, candidates, behav_keys, behav_values, w_query, w_hidden, w_out, clicks):
    users, per_dev, width = candidates.shape
    length = behav_keys.shape[1]
    feats, hid = w_hidden.shape
    nc = ns // 2
    hbm_spec = pl.BlockSpec(memory_space=pltpu.HBM)
    vmem_spec = pl.BlockSpec(memory_space=pltpu.VMEM)
    logits, grad_hidden, grad_out = pl.pallas_call(
        functools.partial(kernel, nc, ng),
        out_shape=(
            jax.ShapeDtypeStruct((per_dev, users), F32),
            jax.ShapeDtypeStruct((feats, hid), F32),
            jax.ShapeDtypeStruct((8, width), F32),
        ),
        in_specs=[hbm_spec] * 7,
        out_specs=(vmem_spec, vmem_spec, vmem_spec),
        scratch_shapes=[
            pltpu.VMEM((2, ns, 16, width), BF16),
            pltpu.VMEM((ns * 16, width), F32),
            pltpu.VMEM((2, ns * 16, width), F32),
            pltpu.VMEM((users, length, width), BF16),
            pltpu.VMEM((users, length, width), BF16),
            pltpu.VMEM((length, HEADS * width), F32),
            pltpu.VMEM((length, HEADS * width), F32),
            pltpu.VMEM((HEADS * width, width), BF16),
            pltpu.VMEM((width, width), BF16),
            pltpu.VMEM((feats, hid), BF16),
            pltpu.VMEM((1, hid), F32),
            pltpu.VMEM((per_dev, users), jnp.int32),
            pltpu.VMEM((per_dev, users, width), F32),
            pltpu.VMEM((users, 2, 2, 64, width), F32),
            pltpu.VMEM((users, 2, 64, width), F32),
            pltpu.VMEM((nc, 40, width), F32),
            pltpu.VMEM((nc, 40, width), F32),
            pltpu.VMEM((64, width), F32),
            pltpu.VMEM((64, width), F32),
            pltpu.VMEM((2, nc, 16, width), BF16),
            pltpu.VMEM((2, nc, 16, width), BF16),
            pltpu.VMEM((2, ng, 16, width), BF16),
            pltpu.VMEM((2, 2, nc, 16, width), BF16),
            pltpu.VMEM((nc, 1, width), F32),
            pltpu.VMEM((nc, 1, width), F32),
            pltpu.VMEM((4, 8, width), F32),
            pltpu.VMEM((ng, 8, width), F32),
            pltpu.VMEM((8, 8, width), F32),
            pltpu.VMEM((2, 8, width), F32),
            pltpu.SemaphoreType.DMA((2, users)),
            pltpu.SemaphoreType.DMA((6,)),
            pltpu.SemaphoreType.DMA((users,)),
            pltpu.SemaphoreType.DMA,
            pltpu.SemaphoreType.DMA((PHASES,)),
            pltpu.SemaphoreType.DMA((PHASES,)),
        ],
        compiler_params=pltpu.CompilerParams(
            collective_id=0, has_side_effects=True, vmem_limit_bytes=40 * 2**20
        ),
        name="ranker",
    )(
        *(
            pltpu.with_memory_space_constraint(operand, pltpu.HBM)
            for operand in (
                candidates.reshape(users * per_dev, width),
                behav_keys,
                behav_values,
                w_query,
                w_hidden,
                w_out.reshape(1, hid),
                jnp.transpose(clicks),
            )
        )
    )
    return jnp.transpose(logits), grad_hidden, grad_out.reshape(hid)


def solution(mesh):
    return jax.shard_map(
        functools.partial(on_device, mesh.shape["seq"], mesh.shape["grp"]),
        mesh=mesh,
        in_specs=(
            P("grp", "seq", None),
            P("grp", "seq", None),
            P("grp", "seq", None),
            P(),
            P(),
            P(),
            P("grp", "seq"),
        ),
        out_specs=(P("grp", "seq"), P(), P()),
        check_vma=False,
    )
```

profile of v0, /device:TPU:1, one launch (start us, length us, event | category | flops | bytes accessed | tf_op | source)
XLA Modules:
  0.0 63.5 jit_solution(10448414406560444725)
XLA Ops:
  0.6 60.7 %ranker.1 = (f32[2,16]{1,0:T(2,128)S(1)}, f32[256,1024]{1,0:T(8,128)S(1)}, f32[8,128]{1,0:T(8,128)S(1)}) custom-call(bf16[32,128]{1,0:T(8,128)(2,1)} %bitcast.7, bf16[16,1024,128]{2,1,0:T(8,128)(2,1)} %keys_hbm.1, bf16[16,1024,128]{2,1,0:T(8,128)(2,1)} %vals_hbm.1, bf16[128,128]{1,0:T(8,128)(2,1)} %wq_hbm.1, bf16[256,1024]{1,0:T(8,128)(2,1)} %wh_hbm.1, ...), custom_call_target="tpu_custom_call" | custom-call | tf_op jit(solution)/shard_map/ranker/pallas_call | solution.py:517
  61.4 0.6 copy.13
  61.9 1.0 %copy.14 = f32[256,1024]{1,0:T(8,128)} copy(f32[256,1024]{1,0:T(8,128)S(1)} %get-tuple-element.13) | data formatting | bytes 2097152
  62.9 0.6 copy.15
where the time goes:
time: 63.6 us; the launch traced here: 63.5 us
  Pallas kernels  60.7 us (95%)
  local copies, waits for them, and re-layouts  2.13 us (3%)
  between operations  0.64 us (1%)
    pallas_call x1, Pallas kernels, on_device(): pl.pallas_call(functools.partial(kernel, nc, ng), out_shape=(jax.ShapeDty...  60.7 us
    unnamed x3, local copies, waits for them, and re-layouts  2.13 us

commit v1 on v0

--- a/solution.py
+++ b/solution.py
@@ -82,8 +82,12 @@
     hw = HEADS * width
 
     def user_at(t):
+        turn = lax.rem(t, half_users)
+        offset = 0
+        for place, step in enumerate((4, 3, 5, 1, 7, 2, 6, 0)):
+            offset = jnp.where(turn == place, step, offset)
         return lax.rem(first_half + t // half_users, 2) * half_users + lax.rem(
-            u_me + 1 + t, half_users
+            u_me + offset, half_users
         )
 
     def on_chip(k):
@@ -114,6 +118,23 @@
     def wait_recv(ref, phase):
         local(ref, ref, recv_sems.at[phase]).wait()
 
+    barrier = pltpu.get_barrier_semaphore()
+    pl.semaphore_signal(barrier, inc=1, device_id={"seq": twin}, device_id_type=MESH)
+
+    @pl.loop(1, nc)
+    def _(k):
+        pl.semaphore_signal(
+            barrier, inc=1, device_id={"seq": same_core(on_chip(k))}, device_id_type=MESH
+        )
+
+    for k in range(1, ng):
+        pl.semaphore_signal(
+            barrier,
+            inc=1,
+            device_id={"seq": me, "grp": lax.rem(grp + k, ng)},
+            device_id_type=MESH,
+        )
+
     own_loads = [
         local(cand_hbm.at[pl.ds(16 * i, 16)], x_buf.at[i, core * nc + chip], w_sems.at[i])
         for i in range(2)
@@ -135,23 +156,6 @@
     wh_load.start()
     wout_load = local(wout_hbm, wout_ref, w_sems.at[5])
     wout_load.start()
-
-    barrier = pltpu.get_barrier_semaphore()
-    pl.semaphore_signal(barrier, inc=1, device_id={"seq": twin}, device_id_type=MESH)
-
-    @pl.loop(1, nc)
-    def _(k):
-        pl.semaphore_signal(
-            barrier, inc=1, device_id={"seq": same_core(on_chip(k))}, device_id_type=MESH
-        )
-
-    for k in range(1, ng):
-        pl.semaphore_signal(
-            barrier,
-            inc=1,
-            device_id={"seq": me, "grp": lax.rem(grp + k, ng)},
-            device_id_type=MESH,
-        )
 
     clicks_load.wait()
     row_u = lax.broadcasted_iota(jnp.int32, (users, users), 0)
@@ -423,18 +427,6 @@
         to = at_zy * 4 + lax.rem(at_x + k, 4)
         remote(o1.at[at_x], o1.at[at_x], OUT_X, same_core(to)).start()
 
-    wide = jnp.broadcast_to(logits, (nc, width))
-    for i in range(nc):
-        l_send[i] = wide[i : i + 1, :]
-    l_slot = c_me * users + u_me
-
-    @pl.loop(1, nc)
-    def _(k):
-        to = on_chip(k)
-        remote(l_send.at[to], l_recv.at[l_slot], LOGITS, same_core(to)).start()
-
-    l_recv[l_slot] = l_send[chip]
-
     wait_recv(o1.at[pl.ds(0, 3)], OUT_X)
     o2[grp] = o1[0] + o1[1] + o1[2] + o1[3]
     for k in range(1, ng):
@@ -450,6 +442,18 @@
     for k in range(1, 8):
         to = lax.rem(at_zy + k, 8) * 4 + at_x
         remote(o3.at[at_zy], o3.at[at_zy], OUT_ZY, same_core(to)).start()
+    wide = jnp.broadcast_to(logits, (nc, width))
+    for i in range(nc):
+        l_send[i] = wide[i : i + 1, :]
+    l_slot = c_me * users + u_me
+
+    @pl.loop(1, nc)
+    def _(k):
+        to = on_chip(k)
+        remote(l_send.at[to], l_recv.at[l_slot], LOGITS, same_core(to)).start()
+
+    l_recv[l_slot] = l_send[chip]
+
     for part in range(2):
         wait_recv(z_buf.at[part, pl.ds(0, ng - 1)], GRP + part)
         ga_buf[part, core, chip] = jnp.sum(z_buf[part].astype(F32), axis=0).astype(BF16)

time: 63.6 us -> 63.1 us (level)
  no operation moved by 1% of the time
where the time goes in v1:
time: 63.1 us; the launch traced here: 63 us
  Pallas kernels  60.2 us (95%)
  local copies, waits for them, and re-layouts  2.13 us (3%)
  between operations  0.64 us (1%)
    pallas_call x1, Pallas kernels, on_device(): pl.pallas_call(functools.partial(kernel, nc, ng), out_shape=(jax.ShapeDty...  60.2 us
    unnamed x3, local copies, waits for them, and re-layouts  2.13 us

profile of v1, /device:TPU:1, one launch (start us, length us, event | category | flops | bytes accessed | tf_op | source)
XLA Modules:
  0.0 63.0 jit_solution(5632266469251421170)
XLA Ops:
  0.6 60.2 %ranker.1 = (f32[2,16]{1,0:T(2,128)S(1)}, f32[256,1024]{1,0:T(8,128)S(1)}, f32[8,128]{1,0:T(8,128)S(1)}) custom-call(bf16[32,128]{1,0:T(8,128)(2,1)} %bitcast.7, bf16[16,1024,128]{2,1,0:T(8,128)(2,1)} %keys_hbm.1, bf16[16,1024,128]{2,1,0:T(8,128)(2,1)} %vals_hbm.1, bf16[128,128]{1,0:T(8,128)(2,1)} %wq_hbm.1, bf16[256,1024]{1,0:T(8,128)(2,1)} %wh_hbm.1, ...), custom_call_target="tpu_custom_call" | custom-call | tf_op jit(solution)/shard_map/ranker/pallas_call | solution.py:521
  60.8 0.6 copy.13
  61.4 1.0 %copy.14 = f32[256,1024]{1,0:T(8,128)} copy(f32[256,1024]{1,0:T(8,128)S(1)} %get-tuple-element.13) | data formatting | bytes 2097152
  62.4 0.6 copy.15
